TPU v7x, 32 devices: a whole 2x2x4 slice. The times are simulated.
32 devices in a mesh: src: 4 (over y, x), rcv: 8 (over z, core).
Axes of the slice: x: 2, y: 2, z: 4, core: 2. Of those that a mesh axis runs over, the one named last changes fastest.
Arguments:
- traces: float32 [512, 512, 1024], P('src', 'rcv'), may hold values from -6 to 6
- freq_index: int32 [256], replicated, may hold values from 1 to 511, as said below
- primaries: float32 [256, 2, 512, 512], P(('src', 'rcv')), may hold values from -0.1875 to 0.1875
Outputs:
- residual: float32 [256, 2, 512, 512], P(('src', 'rcv'))
- residual_next: float32 [256, 2, 512, 512], P(('src', 'rcv'))
Inputs may be any that keep to these rules, and one draw needn't show every extreme that they name: `freq_index`: sorted ascending; repeats possible; the first is 1 and the last is 511.
All inputs are finite; a program needn't handle non-finite values.
Results may differ from a plain program's by a relative error of at most 0.00012.
Values sent between devices are 32-bit elements; how exact they have to be, the bound alone decides.
No kernel may reach another device: no remote copies, remote signals or barrier semaphores. Data moves between devices by JAX's collectives and lax.ppermute only.
A program may use at most 256 MiB of HBM per device.

v0:
```python
import math

import jax
import jax.numpy as jnp
from jax import lax
from jax.sharding import PartitionSpec as P


def freq_table(freq_index, samples):
    times = jnp.arange(samples, dtype=jnp.int32)
    phase = freq_index[:, None] * times[None, :] % samples
    angle = phase.astype(jnp.float32) * (2.0 * math.pi / samples)
    return jnp.stack([jnp.cos(angle), -jnp.sin(angle)], axis=1) / math.sqrt(samples)


def matrix_product(left, right):
    return jnp.einsum("fij,fjk->fik", left, right, precision=lax.Precision.HIGHEST)


def complex_product(left_re, left_im, right_re, right_im, adjoint):
    if adjoint:
        right_re = jnp.swapaxes(right_re, 1, 2)
        right_im = -jnp.swapaxes(right_im, 1, 2)
    real_part = matrix_product(left_re, right_re) - matrix_product(left_im, right_im)
    imag_part = matrix_product(left_re, right_im) + matrix_product(left_im, right_re)
    return (real_part, imag_part)


def on_device(traces, freq_index, primaries):
    src_local, rcv_local, samples = traces.shape
    n_src = lax.axis_size("src")
    n_rcv = lax.axis_size("rcv")
    table = freq_table(freq_index, samples)
    flat = traces.reshape(src_local * rcv_local, samples)
    spectrum = lax.dot_general(
        table,
        flat,
        (((2,), (1,)), ((), ())),
        precision=lax.Precision.HIGHEST,
        preferred_element_type=jnp.float32,
    )
    spectrum = spectrum[None]
    freq_local = primaries.shape[0]
    arrived = lax.all_to_all(spectrum, ("src", "rcv"), split_axis=1, concat_axis=0, tiled=True)
    arrived = arrived.reshape(n_src, n_rcv, freq_local, 2, src_local, rcv_local)
    arrived = jnp.transpose(arrived, (2, 3, 0, 4, 1, 5))
    whole = arrived.reshape(freq_local, 2, n_src * src_local, n_rcv * rcv_local)
    data_re = 0.5 * (whole[:, 0] + jnp.swapaxes(whole[:, 0], 1, 2))
    data_im = 0.5 * (whole[:, 1] + jnp.swapaxes(whole[:, 1], 1, 2))
    model_re, model_im = complex_product(primaries[:, 0], primaries[:, 1], data_re, data_im, False)
    resid_re = data_re - model_re
    resid_im = data_im - model_im
    grad_re, grad_im = complex_product(resid_re, resid_im, data_re, data_im, True)
    pred_re, pred_im = complex_product(grad_re, grad_im, data_re, data_im, False)
    offset = (lax.axis_index("src") * n_rcv + lax.axis_index("rcv")) * freq_local
    weights = freq_index.astype(jnp.float32) / (samples // 2)
    weights = lax.dynamic_slice_in_dim(weights, offset, freq_local)
    scaled = weights[:, None, None]
    numer = jnp.sum(scaled * (resid_re * pred_re + resid_im * pred_im))
    denom = jnp.sum(scaled * (pred_re * pred_re + pred_im * pred_im))
    numer, denom = lax.psum((numer, denom), ("src", "rcv"))
    step_size = numer / denom
    resid = jnp.stack([resid_re, resid_im], 1)
    pred = jnp.stack([pred_re, pred_im], 1)
    return (resid, resid - step_size * pred)


def solution(mesh):
    in_specs = (P("src", "rcv", None), P(), P(("src", "rcv"), None, None, None))
    out_specs = (P(("src", "rcv"), None, None, None), P(("src", "rcv"), None, None, None))
    return jax.shard_map(
        on_device, mesh=mesh, in_specs=in_specs, out_specs=out_specs, check_vma=False
    )
```

profile of v0, /device:TPU:0, one launch (start us, length us, event | category | flops | bytes accessed | tf_op | source)
XLA Modules:
  0.0 993.2 jit_solution(14824239951726077147)
XLA Ops:
  0.6 4.9 fusion.46
  5.5 58.5 %convolution_bitcast_fusion = f32[1,256,2,8192]{3,1,2,0:T(8,128)S(1)} fusion(f32[8192,1024,1]{1,0,2:T(8,128)} %bitcast.78, f32[256,1,1024]{2,0,1:T(8,128)S(1)} %get-tuple-element.19, f32[256,1,1024]{2,0,1:T(8,128)S(1)} %get-tuple-element.18), kind=kOutput, calls=%fused_computation.3 | convolution fusion | flops 51540656128 | bytes 52428800 | tf_op jit(solution)/shard_map/dot_general | solution.py:35
  64.0 14.7 %copy.54 = f32[1,256,2,8192]{3,2,0,1:T(2,128)} copy(f32[1,256,2,8192]{3,1,2,0:T(8,128)S(1)} %convolution_bitcast_fusion) | data formatting | bytes 33554432 | tf_op jit(solution)/shard_map/broadcast_in_dim | solution.py:42
  78.6 0.0 copy-start.2
  78.7 7.4 all-to-all-start
  86.1 0.0 copy-done.2
  86.1 0.6 dynamic_slice.3
  86.7 364.1 %all-to-all-done = f32[1,256,2,8192]{3,2,0,1:T(2,128)} async-done(((f32[1,256,2,8192]{3,2,0,1:T(2,128)}), f32[1,256,2,8192]{3,2,0,1:T(2,128)}, u32[]{:S(2)}, u32[]{:S(2)}) %all-to-all-start) | async-done | bytes 16777248 | tf_op jit(solution)/shard_map/all_to_all | solution.py:44
  450.8 17.7 %copy.55 = f32[1,256,2,8192]{3,1,2,0:T(8,128)} copy(f32[1,256,2,8192]{3,2,0,1:T(2,128)} %all-to-all-done) | data formatting | bytes 33554432 | tf_op jit(solution)/shard_map/all_to_all | solution.py:44
  468.5 27.0 %reshape.113 = f32[4,8,8,2,128,64]{5,4,2,1,0,3:T(8,128)} reshape(f32[1,256,2,8192]{3,1,2,0:T(8,128)} %copy.55) | data formatting | bytes 33554432 | tf_op jit(solution)/shard_map/reshape | solution.py:45
  495.5 34.0 %copy.97 = f32[8,2,4,128,8,64]{5,4,3,2,0,1:T(8,128)} copy(f32[8,2,4,128,8,64]{5,3,0,4,2,1:T(8,128)} %bitcast.75) | data formatting | bytes 33554432 | tf_op jit(solution)/shard_map/reshape | solution.py:47
  529.5 27.6 %reshape.116 = f32[8,2,512,512]{3,2,0,1:T(8,128)} reshape(f32[8,2,4,128,8,64]{5,4,3,2,0,1:T(8,128)} %copy.97) | data formatting | bytes 33554432 | tf_op jit(solution)/shard_map/reshape | solution.py:47
  557.1 10.9 %slice_bitcast_fusion.1 = (f32[8,512,512]{2,1,0:T(8,128)}, f32[8,512,512]{2,1,0:T(8,128)}) fusion(f32[8,2,512,512]{3,2,0,1:T(8,128)} %reshape.116), kind=kLoop, calls=%fused_computation.21 | loop fusion | bytes 33554432 | tf_op jit(solution)/shard_map/squeeze | solution.py:48
  568.0 9.1 copy.58
  577.1 9.1 copy.61
  586.3 19.4 %fusion.10 = (f32[8,512,512]{1,2,0:T(8,128)}, f32[8,512,512]{1,2,0:T(8,128)}) fusion(f32[8,512,512]{1,2,0:T(8,128)} %copy.58, f32[8,2,512,512]{3,2,0,1:T(8,128)} %reshape.116, f32[8,512,512]{1,2,0:T(8,128)} %copy.61), kind=kLoop, calls=%fused_computation.15 | loop fusion | flops 8388608 | bytes 50331648 | tf_op jit(solution)/shard_map/mul | solution.py:48
  605.6 0.0 copy-start
  605.6 19.6 %fusion.1 = f32[8,512,512]{2,1,0:T(8,128)} fusion(f32[8,512,512]{1,2,0:T(8,128)} %get-tuple-element.14, f32[8,2,512,512]{3,2,1,0:T(8,128)} %param.5), kind=kOutput, calls=%fused_computation.4 | convolution fusion | flops 12884901888 | bytes 25165824 | tf_op jit(solution)/shard_map/fij,fjk->fik/dot_general | solution.py:17
  625.3 0.0 copy-done
  625.3 17.3 %fusion.3 = f32[8,512,512]{2,1,0:T(8,128)} fusion(f32[8,512,512]{1,2,0:T(8,128)S(1)} %copy-done, f32[8,2,512,512]{3,2,1,0:T(8,128)} %param.5), kind=kOutput, calls=%fused_computation.6 | convolution fusion | flops 12884901888 | bytes 25165824 | tf_op jit(solution)/shard_map/fij,fjk->fik/dot_general | solution.py:17
  642.6 42.4 %bitcast_subtract_fusion = f32[8,512,512]{1,2,0:T(8,128)} fusion(f32[8,512,512]{1,2,0:T(8,128)} %get-tuple-element.15, f32[8,512,512]{2,1,0:T(8,128)} %fusion.1, f32[8,2,512,512]{3,2,1,0:T(8,128)} %param.5), kind=kOutput, calls=%fused_computation.16 | convolution fusion | flops 12889096192 | bytes 41943040 | tf_op jit(solution)/shard_map/fij,fjk->fik/dot_general | solution.py:17
  685.0 19.3 %fusion.50 = f32[8,512,512]{2,1,0:T(8,128)} fusion(f32[8,512,512]{1,2,0:T(8,128)} %bitcast_subtract_fusion, f32[8,512,512]{1,2,0:T(8,128)} %get-tuple-element.14), kind=kOutput, calls=%fused_computation.59 | convolution fusion | flops 12884901888 | bytes 25165824 | tf_op jit(solution)/shard_map/fij,fjk->fik/dot_general | solution.py:17
  704.2 42.7 %bitcast_subtract_fusion.1 = f32[8,512,512]{1,2,0:T(8,128)} fusion(f32[8,512,512]{1,2,0:T(8,128)} %get-tuple-element.14, f32[8,512,512]{2,1,0:T(8,128)} %fusion.3, f32[8,2,512,512]{3,2,1,0:T(8,128)} %param.5), kind=kOutput, calls=%fused_computation.17 | convolution fusion | flops 12889096192 | bytes 41943040 | tf_op jit(solution)/shard_map/fij,fjk->fik/dot_general | solution.py:17
  746.9 0.0 slice-start
  746.9 21.7 %fusion.11 = f32[8,512,512]{2,1,0:T(8,128)} fusion(f32[8,512,512]{1,2,0:T(8,128)} %bitcast_subtract_fusion.1, f32[8,512,512]{1,2,0:T(8,128)} %get-tuple-element.15), kind=kOutput, calls=%fused_computation.22 | convolution fusion | flops 12886999040 | bytes 25165824 | tf_op jit(solution)/shard_map/fij,fjk->fik/dot_general | solution.py:17
  768.6 0.0 slice-start.1
  768.6 23.5 %fusion.19 = f32[8,512,512]{1,2,0:T(8,128)} fusion(f32[8,512,512]{1,2,0:T(8,128)} %get-tuple-element.14, f32[8,512,512]{2,1,0:T(8,128)} %fusion.11, f32[8,512,512]{2,1,0:T(8,128)} %fusion.50), kind=kOutput, calls=%fused_computation.30 | convolution fusion | flops 12886999040 | bytes 33554432 | tf_op jit(solution)/shard_map/fij,fjk->fik/dot_general | solution.py:17
  792.1 0.0 slice-done
  792.1 0.0 slice-done.1
  792.1 19.8 %fusion.21 = f32[8,512,512]{1,2,0:T(8,128)} fusion(f32[8,512,512]{1,2,0:T(8,128)S(1)} %bitcast.72, f32[8,512,512]{2,1,0:T(8,128)} %fusion.11, f32[8,512,512]{2,1,0:T(8,128)} %fusion.50), kind=kOutput, calls=%fused_computation.32 | convolution fusion | flops 12886999040 | bytes 33554432 | tf_op jit(solution)/shard_map/fij,fjk->fik/dot_general | solution.py:17
  811.9 17.0 %fusion.13 = f32[8,512,512]{2,1,0:T(8,128)} fusion(f32[8,512,512]{1,2,0:T(8,128)} %bitcast_subtract_fusion, f32[8,512,512]{1,2,0:T(8,128)S(1)} %bitcast.72), kind=kOutput, calls=%fused_computation.24 | convolution fusion | flops 12886999040 | bytes 25165824 | tf_op jit(solution)/shard_map/fij,fjk->fik/dot_general | solution.py:17
  828.9 19.5 %fusion.49 = f32[8,512,512]{2,1,0:T(8,128)} fusion(f32[8,512,512]{1,2,0:T(8,128)} %bitcast_subtract_fusion.1, f32[8,512,512]{1,2,0:T(8,128)} %get-tuple-element.14), kind=kOutput, calls=%fused_computation.58 | convolution fusion | flops 12884901888 | bytes 25165824 | tf_op jit(solution)/shard_map/fij,fjk->fik/dot_general | solution.py:17
  848.4 0.0 copy-start.1
  848.4 21.6 %fusion.31 = f32[8,512,512]{1,2,0:T(8,128)} fusion(f32[8,512,512]{1,2,0:T(8,128)} %fusion.21, f32[8,512,512]{1,2,0:T(8,128)} %get-tuple-element.14, f32[8,512,512]{2,1,0:T(8,128)} %fusion.49, f32[8,512,512]{2,1,0:T(8,128)} %fusion.13), kind=kOutput, calls=%fused_computation.38 | convolution fusion | flops 12889096192 | bytes 41943040 | tf_op jit(solution)/shard_map/fij,fjk->fik/dot_general | solution.py:17
  870.1 0.0 copy-done.1
  870.1 28.1 %multiply_reduce_fusion = (f32[]{:T(128)}, f32[]{:T(128)}, f32[8,512,512]{1,2,0:T(8,128)}) fusion(f32[8,512,512]{1,2,0:T(8,128)} %fusion.31, f32[8]{0:T(128)S(1)} %copy-done.1, f32[8,512,512]{1,2,0:T(8,128)} %bitcast_subtract_fusion, f32[8,512,512]{1,2,0:T(8,128)} %bitcast_subtract_fusion.1, f32[8,512,512]{1,2,0:T(8,128)} %fusion.19, ...), kind=kOutput, calls=%fused_computation.18 | convolution fusion | flops 12910067712 | bytes 67108904 | tf_op jit(solution)/shard_map/fij,fjk->fik/dot_general | solution.py:17
  898.2 37.1 %all-reduce = (f32[]{:T(128)}, f32[]{:T(128)}) all-reduce(f32[]{:T(128)} %get-tuple-element.9, f32[]{:T(128)} %get-tuple-element.8), channel_id=1, replica_groups=mesh['src'=4,'rcv'=8] {'src','rcv'}, use_global_device_ids=true, to_apply=%region_1.2 | all-reduce | flops 2 | bytes 16 | tf_op jit(solution)/shard_map/psum | solution.py:61
  936.5 21.8 %fusion = (f32[8,2,512,512]{2,3,0,1:T(8,128)}, f32[8,2,512,512]{2,3,0,1:T(8,128)}) fusion(f32[8,1,512,512]{2,3,0,1:T(8,128)} %bitcast.77, f32[8,1,512,512]{2,3,0,1:T(8,128)} %bitcast.76, f32[]{:T(128)S(6)} %div.19, f32[8,1,512,512]{2,3,0,1:T(8,128)} %bitcast.73, f32[8,1,512,512]{2,3,0,1:T(8,128)} %bitcast.74), kind=kLoop, calls=%fused_computation.2 | loop fusion | flops 16777216 | bytes 67108864 | tf_op jit(solution)/shard_map/sub | solution.py:65
  958.3 17.3 %copy.79 = f32[8,2,512,512]{3,2,1,0:T(8,128)} copy(f32[8,2,512,512]{2,3,0,1:T(8,128)} %get-tuple-element.13) | data formatting | bytes 33554432
  975.7 17.3 %copy.80 = f32[8,2,512,512]{3,2,1,0:T(8,128)} copy(f32[8,2,512,512]{2,3,0,1:T(8,128)} %get-tuple-element.12) | data formatting | bytes 33554432
  (2 shorter events, 0.0 us)
Async XLA Ops:
  78.6 7.4 copy-start.2
  78.7 372.1 %all-to-all-start = ((f32[1,256,2,8192]{3,2,0,1:T(2,128)}), f32[1,256,2,8192]{3,2,0,1:T(2,128)}, u32[]{:S(2)}, u32[]{:S(2)}) async-start(f32[1,256,2,8192]{3,2,0,1:T(2,128)} %copy.54), calls=%async_computation | async-start | bytes 33554432 | tf_op jit(solution)/shard_map/all_to_all | solution.py:44
  605.6 19.6 %copy-start = (f32[8,512,512]{1,2,0:T(8,128)S(1)}, f32[8,512,512]{1,2,0:T(8,128)}, u32[]{:S(2)}) copy-start(f32[8,512,512]{1,2,0:T(8,128)} %get-tuple-element.15) | copy-start | bytes 25165828
  746.9 45.2 %slice-start = ((s8[8388608]{0:T(1024)(128)(4,1)}), s8[4194304]{0:T(1024)(128)(4,1)S(1)}, s32[]{:S(2)}) async-start(s8[8388608]{0:T(1024)(128)(4,1)} %bitcast.71), calls=%async_computation.1 | async-start | bytes 8388608
  768.6 23.5 %slice-start.1 = ((s8[8388608]{0:T(1024)(128)(4,1)}), s8[4194304]{0:T(1024)(128)(4,1)S(1)}, s32[]{:S(2)}) async-start(s8[8388608]{0:T(1024)(128)(4,1)} %bitcast.71), calls=%async_computation.2 | async-start | bytes 8388608
  848.4 21.6 %copy-start.1 = (f32[8]{0:T(128)S(1)}, f32[8]{0:T(128)}, u32[]{:S(2)}) copy-start(f32[8]{0:T(128)} %dynamic_slice.3) | copy-start | bytes 100
where the time goes:
time: 1000 us; the launch traced here: 993 us
  waiting for transfers between devices  364 us (36%)
  matrix products  351 us (35%)
  local copies, waits for them, and re-layouts  185 us (18%)
  other arithmetic  46.1 us (5%)
  blocking collectives  37.1 us (4%)
    all_to_all x1, waiting for transfers between devices, on_device(): lax.all_to_all(spectrum, ('src', 'rcv'), split_axis=1, concat_axis=0, til...  364 us
    dot_general x12, matrix products, matrix_product(): jnp.einsum('fij,fjk->fik', left, right, precision=lax.Precision.HIGHEST)  292 us
    reshape x2, local copies, waits for them, and re-layouts, on_device(): whole = arrived.reshape(freq_local, 2, n_src * src_local, n_rcv * rcv_local)  61.6 us
    dot_general x1, matrix products, on_device(): lax.dot_general(table, flat, (((2,), (1,)), ((), ())), precision=lax.Prec...  58.5 us
    psum x1, blocking collectives, on_device(): numer, denom = lax.psum((numer, denom), ('src', 'rcv'))  37.1 us
    unnamed x12, local copies, waits for them, and re-layouts  34.7 us
    reshape x1, local copies, waits for them, and re-layouts, on_device(): arrived = arrived.reshape(n_src, n_rcv, freq_local, 2, src_local, rcv_local)  27 us
    sub x1, other arithmetic, on_device(): return (resid, resid - step_size * pred)  21.8 us
  transfers between devices with their start and end apart: 1, of which 1 were waited for; matrix products, arithmetic and copies ran while one was open for 0% of the time, Pallas kernels for 0%

commit v1 on v0

--- a/solution.py
+++ b/solution.py
@@ -1,9 +1,22 @@
+import functools
 import math
 
 import jax
 import jax.numpy as jnp
 from jax import lax
+from jax.experimental import pallas as pl
+from jax.experimental.pallas import tpu as pltpu
 from jax.sharding import PartitionSpec as P
+
+AXES = ("src", "rcv")
+LANES = 128
+COST_SCALE = 100
+STREAMS = 4
+STREAM_ROWS = 4
+VMEM_BYTES = 56 * 1024 * 1024
+UPDATE_VMEM_BYTES = 14 * 1024 * 1024
+F32 = jnp.float32
+BF16 = jnp.bfloat16
 
 
 def freq_table(freq_index, samples):
@@ -26,7 +39,7 @@
     return (real_part, imag_part)
 
 
-def on_device(traces, freq_index, primaries):
+def plain_step(traces, freq_index, primaries):
     src_local, rcv_local, samples = traces.shape
     n_src = lax.axis_size("src")
     n_rcv = lax.axis_size("rcv")
@@ -41,7 +54,7 @@
     )
     spectrum = spectrum[None]
     freq_local = primaries.shape[0]
-    arrived = lax.all_to_all(spectrum, ("src", "rcv"), split_axis=1, concat_axis=0, tiled=True)
+    arrived = lax.all_to_all(spectrum, AXES, split_axis=1, concat_axis=0, tiled=True)
     arrived = arrived.reshape(n_src, n_rcv, freq_local, 2, src_local, rcv_local)
     arrived = jnp.transpose(arrived, (2, 3, 0, 4, 1, 5))
     whole = arrived.reshape(freq_local, 2, n_src * src_local, n_rcv * rcv_local)
@@ -58,16 +71,460 @@
     scaled = weights[:, None, None]
     numer = jnp.sum(scaled * (resid_re * pred_re + resid_im * pred_im))
     denom = jnp.sum(scaled * (pred_re * pred_re + pred_im * pred_im))
-    numer, denom = lax.psum((numer, denom), ("src", "rcv"))
+    numer, denom = lax.psum((numer, denom), AXES)
     step_size = numer / denom
     resid = jnp.stack([resid_re, resid_im], 1)
     pred = jnp.stack([pred_re, pred_im], 1)
     return (resid, resid - step_size * pred)
 
 
+def params(**more):
+    return pltpu.CompilerParams(vmem_limit_bytes=VMEM_BYTES, **more)
+
+
+def cost(flops, moved):
+    return pl.CostEstimate(flops=int(flops) // COST_SCALE, bytes_accessed=int(moved) // COST_SCALE, transcendentals=0)
+
+
+def halves(x):
+    high = x.astype(BF16)
+    return high, (x - high.astype(F32)).astype(BF16)
+
+
+def product(left, right):
+    dot = functools.partial(jnp.dot, preferred_element_type=F32)
+    return dot(left[0], right[0]) + (dot(left[0], right[1]) + dot(left[1], right[0]))
+
+
+def transform_kernel(splits, streams, table_ref, *refs):
+    traces_refs, out_refs = refs[:streams], refs[streams:][-len(splits) :]
+    rows, width, samples = traces_refs[0].shape
+    count = table_ref.shape[0] // 4
+    is_left = lax.broadcasted_iota(jnp.int32, (1, LANES), 1) < width
+    contract = (((1,), (1,)), ((), ()))
+    for stream, traces_ref in enumerate(traces_refs):
+        x = traces_ref[...].reshape(rows * width, samples)
+        high, low = halves(x)
+        first = lax.dot_general(table_ref[...], high, contract, preferred_element_type=F32)
+        second = lax.dot_general(table_ref[: 2 * count], low, contract, preferred_element_type=F32)
+        spectrum = first[: 2 * count] + first[2 * count :] + second
+        for pair in range(rows // 2):
+            cols = slice(pair * LANES, (pair + 1) * LANES)
+            re, im = spectrum[:count, cols], spectrum[count:, cols]
+            even = jnp.where(is_left, re, pltpu.roll(im, width, 1))
+            odd = jnp.where(is_left, pltpu.roll(re, width, 1), im)
+            at = stream * rows + 2 * pair
+            for (start, stop), out_ref in zip(splits, out_refs):
+                out_ref[:, at, :] = even[start:stop]
+                out_ref[:, at + 1, :] = odd[start:stop]
+
+
+def transform(table, traces, sizes, after=()):
+    src_local, rcv_local, samples = traces.shape
+    streams, rows = STREAMS, STREAM_ROWS
+    step = streams * rows
+    splits, start = [], 0
+    for size in sizes:
+        splits.append((start, start + size))
+        start += size
+    return pl.pallas_call(
+        functools.partial(transform_kernel, tuple(splits), streams),
+        grid=(src_local // step,),
+        in_specs=[pl.BlockSpec(table.shape, lambda i: (0, 0))]
+        + [
+            pl.BlockSpec((rows, rcv_local, samples), lambda i, k=k: (streams * i + k, 0, 0))
+            for k in range(streams)
+        ]
+        + [pl.BlockSpec(memory_space=pl.ANY)] * len(after),
+        out_specs=[pl.BlockSpec((size, step, LANES), lambda i: (0, i, 0)) for size in sizes],
+        out_shape=[jax.ShapeDtypeStruct((size, src_local, LANES), F32) for size in sizes],
+        compiler_params=params(),
+        cost_estimate=cost(
+            6 * 2 * start * src_local * rcv_local * samples,
+            4 * traces.size + 4 * start * src_local * LANES,
+        ),
+        name="transform",
+    )(table, *[traces] * streams, *after)
+
+
+def split_table(freqs, samples):
+    table = freq_table(freqs, samples)
+    table = jnp.concatenate([table[:, 0], table[:, 1]], axis=0)
+    high = lax.reduce_precision(table, 8, 7)
+    return jnp.concatenate([high.astype(BF16), (table - high).astype(BF16)], axis=0)
+
+
+def merge_kernel(core_ref, own_ref, other_ref, *refs):
+    blocks = own_ref.shape[1]
+    out_refs = refs[-1:] if len(refs[-1].shape) == 6 else refs[-blocks:]
+    width = LANES // 2
+    is_left = lax.broadcasted_iota(jnp.int32, (1, LANES), 1) < width
+    is_first = core_ref[0] == 0
+    for block in range(blocks):
+        out_ref = out_refs[0].at[0, block] if len(out_refs) == 1 else out_refs[block].at[0]
+        for item in range(own_ref.shape[2]):
+            own, other = own_ref[0, block, item], other_ref[0, block, item]
+            left = jnp.where(is_first, own, other)
+            right = jnp.where(is_first, other, own)
+            out_ref[item, 0] = jnp.where(is_left, left, pltpu.roll(right, width, 1))
+            out_ref[item, 1] = jnp.where(is_left, pltpu.roll(left, width, 1), right)
+
+
+def merge(core, own, other, start, count, by_src, after=()):
+    n_src, n_z, _, rows, _ = own.shape
+    spec = pl.BlockSpec((1, n_z, count, rows, LANES), lambda i, c: (i, 0, start // count, 0, 0))
+    if by_src:
+        out_specs = [pl.BlockSpec((1, n_z, count, 2, rows, LANES), lambda i, c: (i, 0, 0, 0, 0, 0))]
+        out_shape = [jax.ShapeDtypeStruct((n_src, n_z, count, 2, rows, LANES), F32)]
+    else:
+        out_specs = [pl.BlockSpec((1, count, 2, rows, LANES), lambda i, c: (i, 0, 0, 0, 0))] * n_z
+        out_shape = [jax.ShapeDtypeStruct((n_src, count, 2, rows, LANES), F32)] * n_z
+    return pl.pallas_call(
+        merge_kernel,
+        grid_spec=pltpu.PrefetchScalarGridSpec(
+            num_scalar_prefetch=1,
+            grid=(n_src,),
+            in_specs=[spec, spec] + [pl.BlockSpec(memory_space=pl.ANY)] * len(after),
+            out_specs=out_specs,
+        ),
+        out_shape=out_shape,
+        compiler_params=params(),
+        cost_estimate=cost(0, 4 * 4 * n_src * n_z * count * rows * LANES),
+        name="merge",
+    )(core, own, other, *after)
+
+
+def regroup_kernel(*refs):
+    out_ref = refs[-1]
+    blocks = out_ref.shape[1]
+    for b in range(blocks):
+        start = 0
+        for ref in (refs[b], refs[blocks + b]):
+            stop = start + ref.shape[1]
+            out_ref[0, b, start:stop] = ref[0]
+            start = stop
+
+
+def regroup(part, other):
+    n_src, _, *rest = part[0].shape
+    count = part[0].shape[1] + other[0].shape[1]
+    spec = lambda x: pl.BlockSpec((1,) + x.shape[1:], lambda i: (i, 0, 0, 0, 0))
+    return pl.pallas_call(
+        regroup_kernel,
+        grid=(n_src,),
+        in_specs=[spec(x) for x in (*part, *other)],
+        out_specs=pl.BlockSpec((1, len(part), count, *rest), lambda i: (i, 0, 0, 0, 0, 0)),
+        out_shape=jax.ShapeDtypeStruct((n_src, len(part), count, *rest), F32),
+        compiler_params=params(),
+        cost_estimate=cost(0, 8 * len(part) * (part[0].size + other[0].size)),
+        name="regroup",
+    )(*part, *other)
+
+
+def pack_kernel(place_ref, block_ref, *out_refs):
+    size = LANES
+    z = place_ref[1]
+    row = lax.broadcasted_iota(jnp.int32, (size, size), 0)
+    col = lax.broadcasted_iota(jnp.int32, (size, size), 1)
+    blocks = block_ref.shape[0]
+    for offset, out_ref in enumerate(out_refs, 1):
+        for k in range(1, blocks):
+            for part in range(2):
+                start = (2 * (k - 1) + part) * size
+                out_ref[0, start : start + size, :] = block_ref[jnp.bitwise_xor(z, k), offset, 0, part]
+        re, im = block_ref[z, offset, 0, 0], block_ref[z, offset, 0, 1]
+        lower, upper = re + re.T, im + im.T
+        start = 2 * (blocks - 1) * size
+        both = jnp.where(row > col, lower, jnp.where(row < col, upper, re))
+        out_ref[0, start : start + size, :] = both
+        diagonal = jnp.sum(jnp.where(row == col, im, 0.0), axis=0, keepdims=True)
+        out_ref[0, start + size :, :] = jnp.broadcast_to(diagonal, (8, size))
+
+
+def pack(place, blocks):
+    n_src, n_z, count, _, size, _ = blocks.shape
+    rows = (2 * (n_src - 1) + 1) * size + 8
+    return pl.pallas_call(
+        pack_kernel,
+        grid_spec=pltpu.PrefetchScalarGridSpec(
+            num_scalar_prefetch=1,
+            grid=(count,),
+            in_specs=[pl.BlockSpec((n_src, n_z, 1, 2, size, size), lambda j, s: (0, 0, j, 0, 0, 0))],
+            out_specs=[pl.BlockSpec((1, rows, size), lambda j, s: (j, 0, 0))] * (n_z - 1),
+        ),
+        out_shape=[jax.ShapeDtypeStruct((count, rows, size), F32)] * (n_z - 1),
+        compiler_params=params(),
+        cost_estimate=cost(0, 4 * 2 * blocks.size),
+        name="pack",
+    )(place, blocks)
+
+
+def place_packed(u_ref, place_ref, own_ref, *far_refs):
+    size = LANES
+    z = place_ref[1]
+    row = lax.broadcasted_iota(jnp.int32, (size, size), 0)
+    col = lax.broadcasted_iota(jnp.int32, (size, size), 1)
+    blocks = own_ref.shape[0]
+    for part in range(2):
+        for source in range(blocks):
+            u_ref[part, z, source * size : (source + 1) * size, :] = own_ref[source, 0, 0, part]
+    for offset, far_ref in enumerate(far_refs, 1):
+        there = jnp.bitwise_xor(z, offset)
+        for k in range(1, blocks):
+            at = pl.ds(pl.multiple_of(jnp.bitwise_xor(there, k) * size, size), size)
+            for part in range(2):
+                start = (2 * (k - 1) + part) * size
+                u_ref[part, there, at, :] = far_ref[0, start : start + size, :]
+        at = pl.ds(pl.multiple_of(there * size, size), size)
+        start = 2 * (blocks - 1) * size
+        both = far_ref[0, start : start + size, :]
+        diagonal = far_ref[0, start + size : start + size + 1, :]
+        u_ref[0, there, at, :] = jnp.where(row >= col, both, 0.0)
+        u_ref[1, there, at, :] = jnp.where(row < col, both, jnp.where(row == col, diagonal, 0.0))
+
+
+def solve_one(u_ref, data_ref, weight, primaries_ref, resid_ref, pred_ref, sums_ref, is_first, before_ref):
+    size = LANES
+    blocks = u_ref.shape[1]
+    for part in range(2):
+        for i in range(blocks):
+            for k in range(i, blocks):
+                here = slice(i * size, (i + 1) * size)
+                there = slice(k * size, (k + 1) * size)
+                block = 0.5 * (u_ref[part, k, here, :] + u_ref[part, i, there, :].T)
+                data_ref[part, here, there] = block
+                if k > i:
+                    data_ref[part, there, here] = block.T
+    data_re, data_im = data_ref[0], data_ref[1]
+    re, im, both = halves(data_re), halves(data_im), halves(data_re + data_im)
+    prim_re, prim_im = primaries_ref[0, 0], primaries_ref[0, 1]
+    first = product(halves(prim_re), re)
+    second = product(halves(prim_im), im)
+    third = product(halves(prim_re + prim_im), both)
+    resid_re = data_re - (first - second)
+    resid_im = data_im - (third - first - second)
+    resid_ref[0, 0] = resid_re
+    resid_ref[0, 1] = resid_im
+    cross = product(re, im)
+    gram_re = product(re, re) + product(im, im)
+    gram_im = cross - cross.T
+    first = product(halves(resid_re), halves(gram_re))
+    second = product(halves(resid_im), halves(gram_im))
+    third = product(halves(resid_re + resid_im), halves(gram_re + gram_im))
+    pred_re = first - second
+    pred_im = third - first - second
+    pred_ref[0, 0] = pred_re
+    pred_ref[0, 1] = pred_im
+
+    def fold(x):
+        x = x.reshape(x.shape[0] // 8, 8, x.shape[1]).sum(0)
+        return sum(x[:, k * LANES : (k + 1) * LANES] for k in range(x.shape[1] // LANES))
+
+    numer = weight * fold(resid_re * pred_re + resid_im * pred_im)
+    denom = weight * fold(pred_re * pred_re + pred_im * pred_im)
+
+    @pl.when(is_first)
+    def _():
+        sums_ref[...] = jnp.zeros_like(sums_ref) if before_ref is None else before_ref[...]
+
+    sums_ref[0] += numer
+    sums_ref[1] += denom
+
+
+def place_raw(u_ref, place_ref, block_ref):
+    size = LANES
+    z = place_ref[1]
+    for source in range(block_ref.shape[0]):
+        for b in range(block_ref.shape[1]):
+            for part in range(2):
+                rows = slice(source * size, (source + 1) * size)
+                u_ref[part, jnp.bitwise_xor(z, b), rows, :] = block_ref[source, b, 0, part]
+
+
+def solve_kernel(offset, n_arrived, n_before, place_ref, weight_ref, primaries_ref, *refs):
+    before_ref = refs[n_arrived + 2] if n_before else None
+    resid_ref, pred_ref, sums_ref, u_ref, data_ref = refs[-5:]
+    j = pl.program_id(0)
+    if n_arrived == 1:
+        place_raw(u_ref, place_ref, refs[0])
+    else:
+        place_packed(u_ref, place_ref, *refs[:n_arrived])
+    solve_one(u_ref, data_ref, weight_ref[offset + j], primaries_ref, resid_ref, pred_ref, sums_ref, j == 0, before_ref)
+
+
+def solve(place, weights, primaries, arrived, offset, before, after=()):
+    size = LANES
+    _, _, n, m = primaries.shape
+    n_src, n_z, count = arrived[0].shape[:3]
+    freq = pl.BlockSpec((1, 2, n, m), lambda j, s: (offset + j, 0, 0, 0))
+    if len(arrived) == 1:
+        specs = [pl.BlockSpec((n_src, n_z, 1, 2, size, size), lambda j, s: (0, 0, j, 0, 0, 0))]
+    else:
+        specs = [pl.BlockSpec((n_src, 1, 1, 2, size, size), lambda j, s: (0, 0, j, 0, 0, 0))]
+        specs += [pl.BlockSpec((1,) + x.shape[1:], lambda j, s: (j, 0, 0)) for x in arrived[1:]]
+    sums = pl.BlockSpec((2, 8, LANES), lambda j, s: (0, 0, 0))
+    n_before = len(before)
+    anywhere = pl.BlockSpec(memory_space=pl.ANY)
+    at = 3 + len(specs)
+    return pl.pallas_call(
+        functools.partial(solve_kernel, offset, len(specs), n_before),
+        grid_spec=pltpu.PrefetchScalarGridSpec(
+            num_scalar_prefetch=1,
+            grid=(count,),
+            in_specs=[pl.BlockSpec(memory_space=pltpu.SMEM), freq]
+            + specs
+            + ([anywhere, anywhere, sums] if n_before else [])
+            + [anywhere] * len(after),
+            out_specs=[freq, freq, sums],
+            scratch_shapes=[
+                pltpu.VMEM((2, n // size, n, size), F32),
+                pltpu.VMEM((2, n, m), F32),
+            ],
+        ),
+        out_shape=[
+            jax.ShapeDtypeStruct(primaries.shape, F32),
+            jax.ShapeDtypeStruct(primaries.shape, F32),
+            jax.ShapeDtypeStruct((2, 8, LANES), F32),
+        ],
+        input_output_aliases={at: 0, at + 1: 1} if n_before else {},
+        compiler_params=params(),
+        cost_estimate=cost(count * 27 * 2 * n * n * m, count * 4 * 2 * n * m * 4),
+        name="solve",
+    )(place, weights, primaries, *arrived, *before, *after)
+
+
+def update_kernel(sums_ref, resid_ref, pred_ref, out_ref):
+    total = jnp.sum(sums_ref[...], axis=0)
+    step = jnp.sum(total[0], keepdims=True) / jnp.sum(total[1], keepdims=True)
+    out_ref[...] = resid_ref[...] - step[None, None] * pred_ref[...]
+
+
+def update(sums, resid, pred):
+    count, _, n, m = resid.shape
+    rows = pl.BlockSpec((1, 2, n, m), lambda i: (i, 0, 0, 0))
+    return pl.pallas_call(
+        update_kernel,
+        grid=(count,),
+        in_specs=[pl.BlockSpec(sums.shape, lambda i: (0, 0, 0, 0)), rows, rows],
+        out_specs=rows,
+        out_shape=jax.ShapeDtypeStruct(resid.shape, F32),
+        compiler_params=pltpu.CompilerParams(vmem_limit_bytes=UPDATE_VMEM_BYTES),
+        cost_estimate=cost(2 * resid.size, 12 * resid.size),
+        name="update",
+    )(sums, resid, pred)
+
+
+def by_offset(values, n_src, n_rcv):
+    bits = n_rcv.bit_length() - 1
+    rcv = lax.axis_index("rcv")
+    values = values.reshape((n_src,) + (2,) * bits + (-1,))
+    for axis in range(bits):
+        bit = (rcv >> (bits - 1 - axis)) & 1
+        values = jnp.where(bit == 1, jnp.flip(values, axis + 1), values)
+    return values.reshape(n_src, n_rcv // 2, 2, -1)
+
+
+def fence(*arrays):
+    return lax.optimization_barrier(arrays)
+
+
+def chunks_of(freq_local):
+    edges = [k * freq_local // 4 for k in range(5)]
+    return list(zip(edges[:-1], edges[1:]))
+
+
+def paired_step(traces, freq_index, primaries):
+    src_local, rcv_local, samples = traces.shape
+    n_src, n_rcv = lax.axis_size("src"), lax.axis_size("rcv")
+    n_z = n_rcv // 2
+    freq_local = primaries.shape[0]
+    src, rcv = lax.axis_index("src"), lax.axis_index("rcv")
+    z, core = rcv // 2, rcv % 2
+    place = jnp.stack([src, z]).astype(jnp.int32)
+    core_id = core.reshape(1).astype(jnp.int32)
+
+    def along(x, offset):
+        return lax.ppermute(x, "rcv", [(i, i ^ offset) for i in range(n_rcv)])
+
+    def along_src(x):
+        return lax.all_to_all(x, "src", split_axis=0, concat_axis=0, tiled=True)
+
+    def along_z(blocks):
+        return [blocks[0]] + [along(blocks[b], 2 * b) for b in range(1, n_z)]
+
+    chunks = chunks_of(freq_local)
+    freqs = by_offset(freq_index, n_src, n_rcv)
+    freqs = jnp.transpose(freqs, (2, 0, 1, 3))
+
+    def transformed(groups, after=(), swap=True):
+        rows = jnp.concatenate([freqs[..., a:b].reshape(-1) for a, b in groups])
+        sizes = [n_src * n_z * (b - a) for a, b in groups for _ in range(2)]
+        outs = transform(split_table(rows, samples), traces, sizes, after)
+        outs = [x.reshape(n_src, n_z, -1, src_local, LANES) for x in outs]
+        pairs = [(outs[2 * i], outs[2 * i + 1]) for i in range(len(groups))]
+        return [(own, along(away, 1) if swap else away) for own, away in pairs]
+
+    weights = freq_index.astype(jnp.float32) / (samples // 2)
+    weights = lax.dynamic_slice_in_dim(weights, (src * n_rcv + rcv) * freq_local, freq_local)
+
+    a, b, c, d = chunks
+    size = [stop - start for start, stop in chunks]
+    middle = (a[0] + a[1]) // 2
+    a1, a2 = (a[0], middle), (middle, a[1])
+    spec_a1, spec_b, spec_a2, spec_c = transformed([a1, b, a2, c])
+    first_a1 = merge(core_id, *spec_a1, 0, a1[1] - a1[0], False)
+    sent_b = merge(core_id, *spec_b, 0, size[1], True, (first_a1[0],))[0]
+    *first_a1, sent_b = fence(*first_a1, sent_b)
+
+    raw_a1 = along_z(first_a1)
+    arrived_b = along_src(sent_b)
+    first_a2 = merge(core_id, *spec_a2, 0, a2[1] - a2[0], False, (sent_b,))
+    sent_c = merge(core_id, *spec_c, 0, size[2], True, (sent_b,))[0]
+    (spec_d,) = transformed([d], (sent_b,), False)
+    *raw_a1, arrived_b, sent_c, own_d, away_d = fence(*raw_a1, arrived_b, sent_c, *spec_d)
+
+    *first_a2, _ = fence(*first_a2, sent_c)
+    raw_a2 = along_z(first_a2)
+    arrived_c = along_src(sent_c)
+    packed_b = pack(place, arrived_b)
+    sent_d = merge(core_id, own_d, along(away_d, 1), 0, size[3], True)[0]
+    *all_a, arrived_b, arrived_c, sent_d, x, y, w = fence(*raw_a1, *raw_a2, arrived_b, arrived_c, sent_d, *packed_b)
+
+    here_b = along_z([arrived_b, x, y, w])
+    arrived_d = along_src(sent_d)
+    packed_c = pack(place, arrived_c)
+    whole_a = regroup(all_a[:n_z], all_a[n_z:])
+    *here_b, arrived_c, arrived_d, whole_a, x, y, w = fence(*here_b, arrived_c, arrived_d, whole_a, *packed_c)
+
+    here_c = along_z([arrived_c, x, y, w])
+    whole_a = along_src(whole_a)
+    packed_d = pack(place, arrived_d)
+    before = solve(place, weights, primaries, here_b, b[0], ())
+    *here_c, arrived_d, whole_a, x, y, w, r, p, q = fence(*here_c, arrived_d, whole_a, *packed_d, *before)
+
+    here_d = along_z([arrived_d, x, y, w])
+    before = solve(place, weights, primaries, [whole_a], a[0], (r, p, q))
+    before = solve(place, weights, primaries, here_c, c[0], before)
+    *here_d, r, p, q = fence(*here_d, *before)
+    before = solve(place, weights, primaries, here_d, d[0], (r, p, q))
+
+    resid, pred, sums = before
+    n_all = n_src * n_rcv
+    sums = jnp.broadcast_to(sums[None], (n_all,) + sums.shape)
+    sums = lax.all_to_all(sums, AXES, split_axis=0, concat_axis=0, tiled=True)
+    return (resid, update(sums, resid, pred))
+
+
 def solution(mesh):
     in_specs = (P("src", "rcv", None), P(), P(("src", "rcv"), None, None, None))
     out_specs = (P(("src", "rcv"), None, None, None), P(("src", "rcv"), None, None, None))
-    return jax.shard_map(
-        on_device, mesh=mesh, in_specs=in_specs, out_specs=out_specs, check_vma=False
-    )
+    n_src, n_rcv = mesh.shape["src"], mesh.shape["rcv"]
+
+    def step(traces, freq_index, primaries):
+        src_local, rcv_local, _ = traces.shape
+        square = src_local == LANES and 2 * rcv_local == LANES
+        if square and n_src == 4 and n_rcv == 2 * n_src and primaries.shape[0] >= 8:
+            return paired_step(traces, freq_index, primaries)
+        return plain_step(traces, freq_index, primaries)
+
+    return jax.shard_map(step, mesh=mesh, in_specs=in_specs, out_specs=out_specs, check_vma=False)

time: 1000 us -> 500 us (0.50)
  matrix products: 351 us -> 0 us
  waiting for transfers between devices: 364 us -> 157 us
  Pallas kernels: 0 us -> 186 us
  local copies, waits for them, and re-layouts: 185 us -> 23 us
  starting transfers between devices: 7.43 us -> 87.7 us
  other arithmetic: 46.1 us -> 7.78 us
    all_to_all x1 -> x4, waiting for transfers between devices: 364 us -> 6.22 us  [along_src(): return lax.all_to_all(x, 'src', split_axis=0, concat_axis=0, tiled=True)]
    dot_general x13 -> x0, matrix products: 351 us -> none  [the longest x12 292 us: matrix_product(): jnp.einsum('fij,fjk->fik', left, right, precision=lax.Precision.HIGHEST)]
    pallas_call x0 -> x16, Pallas kernels: none -> 186 us  [the longest x4 86.5 us: solve(): pl.pallas_call(functools.partial(solve_kernel, offset, len(specs), n_befo...]
    ppermute x0 -> x20, waiting for transfers between devices: none -> 151 us  [along(): return lax.ppermute(x, 'rcv', [(i, i ^ offset) for i in range(n_rcv)])]
    reshape x3 -> x6, local copies, waits for them, and re-layouts: 88.6 us -> 1.18 us  [the longest x1 0.77 us: by_offset(): values = values.reshape((n_src,) + (2,) * bits + (-1,))]
    ppermute x0 -> x20, starting transfers between devices: none -> 67.1 us  [along(): return lax.ppermute(x, 'rcv', [(i, i ^ offset) for i in range(n_rcv)])]
    psum x1 -> x0, blocking collectives: 37.1 us -> none  [on_device(): numer, denom = lax.psum((numer, denom), ('src', 'rcv'))]
    all_to_all x0 -> x1, blocking collectives: none -> 29.5 us  [paired_step(): sums = lax.all_to_all(sums, AXES, split_axis=0, concat_axis=0, tiled=True)]
  transfers between devices with their start and end apart: 1 -> 24, of which waited for: 1 -> 11; matrix products, arithmetic and copies ran while one was open for 0% -> 1% of each run, Pallas kernels for 0% -> 24%
where the time goes in v1:
time: 500 us; the launch traced here: 493 us
  Pallas kernels  186 us (37%)
  waiting for transfers between devices  157 us (31%)
  starting transfers between devices  87.7 us (18%)
  blocking collectives  29.5 us (6%)
  local copies, waits for them, and re-layouts  23 us (5%)
  other arithmetic  7.78 us (2%)
    ppermute x20, waiting for transfers between devices, along(): return lax.ppermute(x, 'rcv', [(i, i ^ offset) for i in range(n_rcv)])  151 us
    pallas_call x4, Pallas kernels, solve(): pl.pallas_call(functools.partial(solve_kernel, offset, len(specs), n_befo...  86.5 us
    ppermute x20, starting transfers between devices, along(): return lax.ppermute(x, 'rcv', [(i, i ^ offset) for i in range(n_rcv)])  67.1 us
    pallas_call x2, Pallas kernels, transform(): pl.pallas_call(functools.partial(transform_kernel, tuple(splits), streams...  51.3 us
    all_to_all x1, blocking collectives, paired_step(): sums = lax.all_to_all(sums, AXES, split_axis=0, concat_axis=0, tiled=True)  29.5 us
    pallas_call x5, Pallas kernels, merge(): pl.pallas_call(merge_kernel, grid_spec=pltpu.PrefetchScalarGridSpec(num_s...  23.5 us
    all_to_all x4, starting transfers between devices, along_src(): return lax.all_to_all(x, 'src', split_axis=0, concat_axis=0, tiled=True)  20.6 us
    unnamed x40, local copies, waits for them, and re-layouts  19.7 us
  transfers between devices with their start and end apart: 24, of which 11 were waited for; matrix products, arithmetic and copies ran while one was open for 1% of the time, Pallas kernels for 24%

profile of v1, /device:TPU:0, one launch (start us, length us, event | category | flops | bytes accessed | tf_op | source)
XLA Modules:
  0.0 492.7 jit_solution(7978488431284969691)
XLA Ops:
  2.5 3.2 fusion.8
  7.7 31.8 %transform.2 = (f32[16,128,128]{2,1,0:T(8,128)}, f32[16,128,128]{2,1,0:T(8,128)}, f32[32,128,128]{2,1,0:T(8,128)}, f32[32,128,128]{2,1,0:T(8,128)}, f32[16,128,1...) custom-call(bf16[768,1024]{1,0:T(8,128)(2,1)} %pad_maximum_fusion.1.table_ref, ...), custom_call_target="tpu_custom_call" | custom-call | flops 193273536 | bytes 461373 | tf_op jit(solution)/shard_map/transform/pallas_call | solution.py:130
  40.1 5.4 %collective-permute-done.other_ref = f32[4,4,1,128,128]{4,3,2,1,0:T(8,128)S(1)} collective-permute-done((f32[4,4,1,128,128]{4,3,2,1,0:T(8,128)}, f32[4,4,1,128,128]{4,3,2,1,0:T(8,128)S(1)}, u32[]{:S(2)}, u32[]{:S(2)}) %collective-permute-start) | collective-permute-done | bytes 1048608 | tf_op jit(solution)/shard_map/ppermute | solution.py:447
  46.5 4.0 merge.5
  50.5 1.4 copy-done.3
  51.9 5.2 %merge.6.refs_0_.refs_4_ = f32[4,4,2,2,128,128]{5,4,3,2,1,0:T(8,128)} custom-call(s32[1]{0:T(128)} %bitcast.2.core_ref, f32[4,4,2,128,128]{4,3,2,1,0:T(8,128)} %bitcast.26, f32[4,4,2,128,128]{4,3,2,1,0:T(8,128)} %copy-done.3, f32[4,1,2,128,128]{4,3,2,1,0:T(8,128)} %get-tuple-element.145.refs_0_), custom_call_target="tpu_custom_call" | custom-call | bytes 83886 | tf_op jit(solution)/shard_map/merge/pallas_call | solution.py:182
  57.1 5.7 %all-to-all-start = ((f32[4,4,2,2,128,128]{5,4,3,2,1,0:T(8,128)}), f32[4,4,2,2,128,128]{5,4,3,2,1,0:T(8,128)}, u32[]{:S(2)}, u32[]{:S(2)}) async-start(f32[4,4,2,2,128,128]{5,4,3,2,1,0:T(8,128)} %merge.6.refs_0_.refs_4_), calls=%async_computation | async-start | bytes 8388608 | tf_op jit(solution)/shard_map/all_to_all | solution.py:450
  64.2 2.8 collective-permute-start.2
  67.0 2.6 collective-permute-start.3
  70.6 1.4 copy-done.2
  72.0 5.2 %merge.7 = f32[4,4,2,2,128,128]{5,4,3,2,1,0:T(8,128)} custom-call(s32[1]{0:T(128)} %bitcast.2.core_ref, f32[4,4,2,128,128]{4,3,2,1,0:T(8,128)} %bitcast.25, f32[4,4,2,128,128]{4,3,2,1,0:T(8,128)} %copy-done.2, f32[4,4,2,2,128,128]{5,4,3,2,1,0:T(8,128)} %merge.6.refs_0_.refs_4_), custom_call_target="tpu_custom_call" | custom-call | bytes 83886 | tf_op jit(solution)/shard_map/merge/pallas_call | solution.py:182
  77.2 19.5 %transform.3 = (f32[32,128,128]{2,1,0:T(8,128)}, f32[32,128,128]{2,1,0:T(8,128)}) custom-call(bf16[256,1024]{1,0:T(8,128)(2,1)} %pad_maximum_fusion.3.table_ref, f32[128,64,1024]{2,1,0:T(8,128)} %refs_3_.3, f32[128,64,1024]{2,1,0:T(8,128)} %refs_3_.3, f32[128,64,1024]{2,1,0:T(8,128)} %refs_3_.3, f32[128,64,1024]{2,1,0:T(8,128)} %refs_3_.3, ...), custom_call_target="tpu_custom_call" | custom-call | flops 64424508 | bytes 377487 | tf_op jit(solution)/shard_map/transform/pallas_call | solution.py:130
  96.7 8.7 %collective-permute-done.3.refs_2_ = f32[4,1,2,128,128]{4,3,2,1,0:T(8,128)S(1)} collective-permute-done((f32[4,1,2,128,128]{4,3,2,1,0:T(8,128)}, f32[4,1,2,128,128]{4,3,2,1,0:T(8,128)S(1)}, u32[]{:S(2)}, u32[]{:S(2)}) %collective-permute-start.3) | collective-permute-done | bytes 524320 | tf_op jit(solution)/shard_map/ppermute | solution.py:447
  105.4 6.2 %all-to-all-done.block_ref.refs_0_ = f32[4,4,2,2,128,128]{5,4,3,2,1,0:T(8,128)} async-done(((f32[4,4,2,2,128,128]{5,4,3,2,1,0:T(8,128)}), f32[4,4,2,2,128,128]{5,4,3,2,1,0:T(8,128)}, u32[]{:S(2)}, u32[]{:S(2)}) %all-to-all-start) | async-done | bytes 4194336 | tf_op jit(solution)/shard_map/all_to_all | solution.py:450
  111.6 4.9 all-to-all-start.1
  117.1 5.4 %collective-permute-done.6.other_ref = f32[4,4,1,128,128]{4,3,2,1,0:T(8,128)S(1)} collective-permute-done((f32[4,4,1,128,128]{4,3,2,1,0:T(8,128)}, f32[4,4,1,128,128]{4,3,2,1,0:T(8,128)S(1)}, u32[]{:S(2)}, u32[]{:S(2)}) %collective-permute-start.6) | collective-permute-done | bytes 1048608 | tf_op jit(solution)/shard_map/ppermute | solution.py:447
  123.4 4.0 merge.8
  127.4 4.8 collective-permute-start.7
  133.3 1.4 collective-permute-start.9
  135.3 4.2 pack.3
  139.5 1.4 copy-done.4
  140.9 5.2 %merge.9 = f32[4,4,2,2,128,128]{5,4,3,2,1,0:T(8,128)} custom-call(s32[1]{0:T(128)} %bitcast.2.core_ref, f32[4,4,2,128,128]{4,3,2,1,0:T(8,128)} %bitcast.27, f32[4,4,2,128,128]{4,3,2,1,0:T(8,128)} %copy-done.4), custom_call_target="tpu_custom_call" | custom-call | bytes 83886 | tf_op jit(solution)/shard_map/merge/pallas_call | solution.py:182
  146.1 9.2 %collective-permute-done.7.refs_5_ = f32[4,1,2,128,128]{4,3,2,1,0:T(8,128)S(1)} collective-permute-done((f32[4,1,2,128,128]{4,3,2,1,0:T(8,128)}, f32[4,1,2,128,128]{4,3,2,1,0:T(8,128)S(1)}, u32[]{:S(2)}, u32[]{:S(2)}) %collective-permute-start.7) | collective-permute-done | bytes 524320 | tf_op jit(solution)/shard_map/ppermute | solution.py:447
  155.3 15.3 %collective-permute-done.8.refs_6_ = f32[4,1,2,128,128]{4,3,2,1,0:T(8,128)S(1)} collective-permute-done((f32[4,1,2,128,128]{4,3,2,1,0:T(8,128)}, f32[4,1,2,128,128]{4,3,2,1,0:T(8,128)S(1)}, u32[]{:S(2)}, u32[]{:S(2)}) %collective-permute-start.8) | collective-permute-done | bytes 524320 | tf_op jit(solution)/shard_map/ppermute | solution.py:447
  171.4 4.8 all-to-all-start.2
  176.3 10.3 %collective-permute-start.11 = (f32[2,904,128]{2,1,0:T(8,128)}, f32[2,904,128]{2,1,0:T(8,128)}, u32[]{:S(2)}, u32[]{:S(2)}) collective-permute-start(f32[2,904,128]{2,1,0:T(8,128)} %get-tuple-element.140), channel_id=1, source_target_pairs={{0,2},{1,3},{2,0},{3,1},{4,6},{5,7},{6,4},{7,5},{8,10},{9,11},{10,... | collective-permute-start | bytes 2777096 | tf_op jit(solution)/shard_map/ppermute | solution.py:447
  187.6 1.4 collective-permute-start.13
  189.1 4.2 pack.4
  193.3 4.7 regroup.1
  198.0 27.3 %collective-permute-done.11.refs_1_ = f32[2,904,128]{2,1,0:T(8,128)} collective-permute-done((f32[2,904,128]{2,1,0:T(8,128)}, f32[2,904,128]{2,1,0:T(8,128)}, u32[]{:S(2)}, u32[]{:S(2)}) %collective-permute-start.11) | collective-permute-done | bytes 925728 | tf_op jit(solution)/shard_map/ppermute | solution.py:447
  225.3 25.3 %collective-permute-done.12.refs_2_ = f32[2,904,128]{2,1,0:T(8,128)} collective-permute-done((f32[2,904,128]{2,1,0:T(8,128)S(1)}, f32[2,904,128]{2,1,0:T(8,128)}, u32[]{:S(2)}, u32[]{:S(2)}) %collective-permute-start.12) | collective-permute-done | bytes 925728 | tf_op jit(solution)/shard_map/ppermute | solution.py:447
  250.7 5.2 %all-to-all-start.3 = ((f32[4,4,2,2,128,128]{5,4,3,2,1,0:T(8,128)}), f32[4,4,2,2,128,128]{5,4,3,2,1,0:T(8,128)}, u32[]{:S(2)}, u32[]{:S(2)}) async-start(f32[4,4,2,2,128,128]{5,4,3,2,1,0:T(8,128)} %regroup.1), calls=%async_computation.3 | async-start | bytes 8388608 | tf_op jit(solution)/shard_map/all_to_all | solution.py:450
  255.9 18.2 %collective-permute-start.14 = (f32[2,904,128]{2,1,0:T(8,128)}, f32[2,904,128]{2,1,0:T(8,128)S(1)}, u32[]{:S(2)}, u32[]{:S(2)}) collective-permute-start(f32[2,904,128]{2,1,0:T(8,128)} %get-tuple-element.157), channel_id=1, source_target_pairs={{0,2},{1,3},{2,0},{3,1},{4,6},{5,7},{6,4},{7,5},{8,10},{9,11},{10,... | collective-permute-start | bytes 2777096 | tf_op jit(solution)/shard_map/ppermute | solution.py:447
  275.2 1.4 collective-permute-start.16
  277.2 4.2 pack.5
  281.4 21.4 %solve.4 = (f32[8,2,512,512]{3,2,1,0:T(8,128)}, f32[8,2,512,512]{3,2,1,0:T(8,128)}, f32[2,8,128]{2,1,0:T(8,128)}) custom-call(s32[2]{0:T(128)} %pad_add_fusion.1.place_ref, f32[8]{0:T(128)} %dynamic_slice.3.weight_ref, f32[8,2,512,512]{3,2,1,0:T(8,128)} %primaries_ref.7, f32[4,4,2,2,128,128]{5,4,3,2,1,0:T(8,128)} %all-to-all-done.block_ref.refs_0_, ...), custom_call_target="tpu_custom_call" | custom-call | flops 144955152 | bytes 167772 | tf_op jit(solution)/shard_map/solve/pallas_call | solution.py:369
  302.8 8.2 %collective-permute-done.14.refs_1_ = f32[2,904,128]{2,1,0:T(8,128)S(1)} collective-permute-done((f32[2,904,128]{2,1,0:T(8,128)}, f32[2,904,128]{2,1,0:T(8,128)S(1)}, u32[]{:S(2)}, u32[]{:S(2)}) %collective-permute-start.14) | collective-permute-done | bytes 925728 | tf_op jit(solution)/shard_map/ppermute | solution.py:447
  311.0 27.4 %collective-permute-done.15.refs_2_ = f32[2,904,128]{2,1,0:T(8,128)S(1)} collective-permute-done((f32[2,904,128]{2,1,0:T(8,128)}, f32[2,904,128]{2,1,0:T(8,128)S(1)}, u32[]{:S(2)}, u32[]{:S(2)}) %collective-permute-start.15) | collective-permute-done | bytes 925728 | tf_op jit(solution)/shard_map/ppermute | solution.py:447
  338.4 17.0 %collective-permute-start.17 = (f32[2,904,128]{2,1,0:T(8,128)}, f32[2,904,128]{2,1,0:T(8,128)S(1)}, u32[]{:S(2)}, u32[]{:S(2)}) collective-permute-start(f32[2,904,128]{2,1,0:T(8,128)} %get-tuple-element.173), channel_id=1, source_target_pairs={{0,2},{1,3},{2,0},{3,1},{4,6},{5,7},{6,4},{7,5},{8,10},{9,11},{10,... | collective-permute-start | bytes 2777096 | tf_op jit(solution)/shard_map/ppermute | solution.py:447
  356.5 1.4 collective-permute-start.19
  357.9 21.7 %solve.5 = (f32[8,2,512,512]{3,2,1,0:T(8,128)}, f32[8,2,512,512]{3,2,1,0:T(8,128)}, f32[2,8,128]{2,1,0:T(8,128)}) custom-call(s32[2]{0:T(128)} %pad_add_fusion.1.place_ref, f32[8]{0:T(128)} %dynamic_slice.3.weight_ref, f32[8,2,512,512]{3,2,1,0:T(8,128)} %primaries_ref.7, ...), custom_call_target="tpu_custom_call", output_to_operand_aliasing={{0}: (4, {}), {1}: (5, {})} | custom-call | flops 144955152 | bytes 167772 | tf_op jit(solution)/shard_map/solve/pallas_call | solution.py:369
  379.6 21.7 %solve.6 = (f32[8,2,512,512]{3,2,1,0:T(8,128)}, f32[8,2,512,512]{3,2,1,0:T(8,128)}, f32[2,8,128]{2,1,0:T(8,128)}) custom-call(s32[2]{0:T(128)} %pad_add_fusion.1.place_ref, f32[8]{0:T(128)} %dynamic_slice.3.weight_ref, f32[8,2,512,512]{3,2,1,0:T(8,128)} %primaries_ref.7, ...), custom_call_target="tpu_custom_call", output_to_operand_aliasing={{0}: (7, {}), {1}: (8, {})} | custom-call | flops 144955152 | bytes 167772 | tf_op jit(solution)/shard_map/solve/pallas_call | solution.py:369
  401.3 18.3 %collective-permute-done.18.refs_2_ = f32[2,904,128]{2,1,0:T(8,128)S(1)} collective-permute-done((f32[2,904,128]{2,1,0:T(8,128)}, f32[2,904,128]{2,1,0:T(8,128)S(1)}, u32[]{:S(2)}, u32[]{:S(2)}) %collective-permute-start.18) | collective-permute-done | bytes 925728 | tf_op jit(solution)/shard_map/ppermute | solution.py:447
  420.9 21.7 %solve.7 = (f32[8,2,512,512]{3,2,1,0:T(8,128)}, f32[8,2,512,512]{3,2,1,0:T(8,128)}, f32[2,8,128]{2,1,0:T(8,128)}) custom-call(s32[2]{0:T(128)} %pad_add_fusion.1.place_ref, f32[8]{0:T(128)} %dynamic_slice.3.weight_ref, f32[8,2,512,512]{3,2,1,0:T(8,128)} %primaries_ref.7, ...), custom_call_target="tpu_custom_call", output_to_operand_aliasing={{0}: (7, {}), {1}: (8, {})} | custom-call | flops 144955152 | bytes 167772 | tf_op jit(solution)/shard_map/solve/pallas_call | solution.py:369
  443.3 29.5 %all_to_all.25.sums_ref = f32[32,2,8,128]{3,2,1,0:T(8,128)S(1)} all-to-all(f32[32,2,8,128]{3,2,1,0:T(8,128)S(1)} %broadcast_in_dim.2), channel_id=1, replica_groups=mesh['src'=4,'rcv'=8] {'src','rcv'}, dimensions={0} | all-to-all | bytes 524288 | tf_op jit(solution)/shard_map/all_to_all | solution.py:514
  472.8 5.8 %copy-done = f32[8,2,512,512]{3,2,1,0:T(8,128)S(1)} copy-done((f32[8,2,512,512]{3,2,1,0:T(8,128)S(1)}, f32[8,2,512,512]{3,2,1,0:T(8,128)}, u32[]{:S(2)}) %copy-start) | copy-done | bytes 16777240
  478.6 5.8 %copy-done.1 = f32[8,2,512,512]{3,2,1,0:T(8,128)S(1)} copy-done((f32[8,2,512,512]{3,2,1,0:T(8,128)S(1)}, f32[8,2,512,512]{3,2,1,0:T(8,128)}, u32[]{:S(2)}) %copy-start.1) | copy-done | bytes 16777240
  484.3 7.9 %update.1 = f32[8,2,512,512]{3,2,1,0:T(8,128)} custom-call(f32[32,2,8,128]{3,2,1,0:T(8,128)S(1)} %all_to_all.25.sums_ref, f32[8,2,512,512]{3,2,1,0:T(8,128)S(1)} %copy-done, f32[8,2,512,512]{3,2,1,0:T(8,128)S(1)} %copy-done.1), custom_call_target="tpu_custom_call" | custom-call | flops 83886 | bytes 503316 | tf_op jit(solution)/shard_map/update/pallas_call | solution.py:405
  (85 shorter events, 17.8 us)
Async XLA Ops:
  39.5 11.0 %collective-permute-start.1 = (f32[4,4,2,128,128]{4,3,2,1,0:T(8,128)}, f32[4,4,2,128,128]{4,3,2,1,0:T(8,128)S(1)}, u32[]{:S(2)}, u32[]{:S(2)}) collective-permute-start(f32[4,4,2,128,128]{4,3,2,1,0:T(8,128)} %bitcast.35), channel_id=1, source_target_pairs={{0,1},{1,0},{2,3},{3,2},{4,5},{5,4},{6,7},{7,6},{8,9},{9,8},{10,11... | collective-permute-start | bytes 6291464 | tf_op jit(solution)/shard_map/ppermute | solution.py:447
  40.0 5.5 %collective-permute-start = (f32[4,4,1,128,128]{4,3,2,1,0:T(8,128)}, f32[4,4,1,128,128]{4,3,2,1,0:T(8,128)S(1)}, u32[]{:S(2)}, u32[]{:S(2)}) collective-permute-start(f32[4,4,1,128,128]{4,3,2,1,0:T(8,128)} %bitcast.37), channel_id=1, source_target_pairs={{0,1},{1,0},{2,3},{3,2},{4,5},{5,4},{6,7},{7,6},{8,9},{9,8},{10,11... | collective-permute-start | bytes 3145736 | tf_op jit(solution)/shard_map/ppermute | solution.py:447
  45.5 1.0 copy-start.6
  50.5 1.4 copy-start.3
  57.1 54.6 %all-to-all-start = ((f32[4,4,2,2,128,128]{5,4,3,2,1,0:T(8,128)}), f32[4,4,2,2,128,128]{5,4,3,2,1,0:T(8,128)}, u32[]{:S(2)}, u32[]{:S(2)}) async-start(f32[4,4,2,2,128,128]{5,4,3,2,1,0:T(8,128)} %merge.6.refs_0_.refs_4_), calls=%async_computation | async-start | bytes 8388608 | tf_op jit(solution)/shard_map/all_to_all | solution.py:450
  62.7 7.9 %collective-permute-start.5 = (f32[4,4,2,128,128]{4,3,2,1,0:T(8,128)}, f32[4,4,2,128,128]{4,3,2,1,0:T(8,128)S(1)}, u32[]{:S(2)}, u32[]{:S(2)}) collective-permute-start(f32[4,4,2,128,128]{4,3,2,1,0:T(8,128)} %bitcast.33), channel_id=1, source_target_pairs={{0,1},{1,0},{2,3},{3,2},{4,5},{5,4},{6,7},{7,6},{8,9},{9,8},{10,11... | collective-permute-start | bytes 6291464 | tf_op jit(solution)/shard_map/ppermute | solution.py:447
  64.2 32.5 %collective-permute-start.2 = (f32[4,1,2,128,128]{4,3,2,1,0:T(8,128)}, f32[4,1,2,128,128]{4,3,2,1,0:T(8,128)S(1)}, u32[]{:S(2)}, u32[]{:S(2)}) collective-permute-start(f32[4,1,2,128,128]{4,3,2,1,0:T(8,128)} %get-tuple-element.110), channel_id=1, source_target_pairs={{0,2},{1,3},{2,0},{3,1},{4,6},{5,7},{6,4},{7,5},{8,10},{9,11},{10,... | collective-permute-start | bytes 1572872 | tf_op jit(solution)/shard_map/ppermute | solution.py:447
  67.0 38.4 %collective-permute-start.3 = (f32[4,1,2,128,128]{4,3,2,1,0:T(8,128)}, f32[4,1,2,128,128]{4,3,2,1,0:T(8,128)S(1)}, u32[]{:S(2)}, u32[]{:S(2)}) collective-permute-start(f32[4,1,2,128,128]{4,3,2,1,0:T(8,128)} %get-tuple-element.111), channel_id=1, source_target_pairs={{0,4},{1,5},{2,6},{3,7},{4,0},{5,1},{6,2},{7,3},{8,12},{9,13},{10,... | collective-permute-start | bytes 1572872 | tf_op jit(solution)/shard_map/ppermute | solution.py:447
  69.6 35.8 %collective-permute-start.4 = (f32[4,1,2,128,128]{4,3,2,1,0:T(8,128)}, f32[4,1,2,128,128]{4,3,2,1,0:T(8,128)}, u32[]{:S(2)}, u32[]{:S(2)}) collective-permute-start(f32[4,1,2,128,128]{4,3,2,1,0:T(8,128)} %get-tuple-element.112), channel_id=1, source_target_pairs={{0,6},{1,7},{2,4},{3,5},{4,2},{5,3},{6,0},{7,1},{8,14},{9,15},{10,... | collective-permute-start | bytes 1572872 | tf_op jit(solution)/shard_map/ppermute | solution.py:447
  70.6 1.4 copy-start.2
  96.7 14.9 %copy-start.13 = (f32[4,1,2,128,128]{4,3,2,1,0:T(8,128)}, f32[4,1,2,128,128]{4,3,2,1,0:T(8,128)S(1)}, u32[]{:S(2)}) copy-start(f32[4,1,2,128,128]{4,3,2,1,0:T(8,128)S(1)} %collective-permute-done.2.refs_1_) | copy-start | bytes 1572868
  105.4 6.2 %copy-start.14 = (f32[4,1,2,128,128]{4,3,2,1,0:T(8,128)}, f32[4,1,2,128,128]{4,3,2,1,0:T(8,128)S(1)}, u32[]{:S(2)}) copy-start(f32[4,1,2,128,128]{4,3,2,1,0:T(8,128)S(1)} %collective-permute-done.3.refs_2_) | copy-start | bytes 1572868
  111.6 59.0 %all-to-all-start.1 = ((f32[4,4,2,2,128,128]{5,4,3,2,1,0:T(8,128)}), f32[4,4,2,2,128,128]{5,4,3,2,1,0:T(8,128)}, u32[]{:S(2)}, u32[]{:S(2)}) async-start(f32[4,4,2,2,128,128]{5,4,3,2,1,0:T(8,128)} %merge.7), calls=%async_computation.1 | async-start | bytes 8388608 | tf_op jit(solution)/shard_map/all_to_all | solution.py:450
  116.5 23.0 %collective-permute-start.10 = (f32[4,4,2,128,128]{4,3,2,1,0:T(8,128)}, f32[4,4,2,128,128]{4,3,2,1,0:T(8,128)S(1)}, u32[]{:S(2)}, u32[]{:S(2)}) collective-permute-start(f32[4,4,2,128,128]{4,3,2,1,0:T(8,128)} %bitcast.34), channel_id=1, source_target_pairs={{0,1},{1,0},{2,3},{3,2},{4,5},{5,4},{6,7},{7,6},{8,9},{9,8},{10,11... | collective-permute-start | bytes 6291464 | tf_op jit(solution)/shard_map/ppermute | solution.py:447
  116.6 5.9 %collective-permute-start.6 = (f32[4,4,1,128,128]{4,3,2,1,0:T(8,128)}, f32[4,4,1,128,128]{4,3,2,1,0:T(8,128)S(1)}, u32[]{:S(2)}, u32[]{:S(2)}) collective-permute-start(f32[4,4,1,128,128]{4,3,2,1,0:T(8,128)} %bitcast.36), channel_id=1, source_target_pairs={{0,1},{1,0},{2,3},{3,2},{4,5},{5,4},{6,7},{7,6},{8,9},{9,8},{10,11... | collective-permute-start | bytes 3145736 | tf_op jit(solution)/shard_map/ppermute | solution.py:447
  122.5 1.0 copy-start.5
  127.4 27.9 %collective-permute-start.7 = (f32[4,1,2,128,128]{4,3,2,1,0:T(8,128)}, f32[4,1,2,128,128]{4,3,2,1,0:T(8,128)S(1)}, u32[]{:S(2)}, u32[]{:S(2)}) collective-permute-start(f32[4,1,2,128,128]{4,3,2,1,0:T(8,128)} %get-tuple-element.130), channel_id=1, source_target_pairs={{0,2},{1,3},{2,0},{3,1},{4,6},{5,7},{6,4},{7,5},{8,10},{9,11},{10,... | collective-permute-start | bytes 1572872 | tf_op jit(solution)/shard_map/ppermute | solution.py:447
  132.2 38.4 %collective-permute-start.8 = (f32[4,1,2,128,128]{4,3,2,1,0:T(8,128)}, f32[4,1,2,128,128]{4,3,2,1,0:T(8,128)S(1)}, u32[]{:S(2)}, u32[]{:S(2)}) collective-permute-start(f32[4,1,2,128,128]{4,3,2,1,0:T(8,128)} %get-tuple-element.131), channel_id=1, source_target_pairs={{0,4},{1,5},{2,6},{3,7},{4,0},{5,1},{6,2},{7,3},{8,12},{9,13},{10,... | collective-permute-start | bytes 1572872 | tf_op jit(solution)/shard_map/ppermute | solution.py:447
  133.3 37.3 %collective-permute-start.9 = (f32[4,1,2,128,128]{4,3,2,1,0:T(8,128)}, f32[4,1,2,128,128]{4,3,2,1,0:T(8,128)}, u32[]{:S(2)}, u32[]{:S(2)}) collective-permute-start(f32[4,1,2,128,128]{4,3,2,1,0:T(8,128)} %get-tuple-element.132), channel_id=1, source_target_pairs={{0,6},{1,7},{2,4},{3,5},{4,2},{5,3},{6,0},{7,1},{8,14},{9,15},{10,... | collective-permute-start | bytes 1572872 | tf_op jit(solution)/shard_map/ppermute | solution.py:447
  139.5 1.4 copy-start.4
  155.3 15.3 %copy-start.15 = (f32[4,1,2,128,128]{4,3,2,1,0:T(8,128)}, f32[4,1,2,128,128]{4,3,2,1,0:T(8,128)S(1)}, u32[]{:S(2)}) copy-start(f32[4,1,2,128,128]{4,3,2,1,0:T(8,128)S(1)} %collective-permute-done.7.refs_5_) | copy-start | bytes 1572868
  170.6 0.8 copy-start.16
  170.6 15.9 %copy-start.19 = (f32[2,904,128]{2,1,0:T(8,128)S(1)}, f32[2,904,128]{2,1,0:T(8,128)}, u32[]{:S(2)}) copy-start(f32[2,904,128]{2,1,0:T(8,128)} %get-tuple-element.141) | copy-start | bytes 2777092
  170.6 17.0 %copy-start.18 = (f32[2,904,128]{2,1,0:T(8,128)S(1)}, f32[2,904,128]{2,1,0:T(8,128)}, u32[]{:S(2)}) copy-start(f32[2,904,128]{2,1,0:T(8,128)} %get-tuple-element.142) | copy-start | bytes 2777092
  171.4 79.3 %all-to-all-start.2 = ((f32[4,4,2,2,128,128]{5,4,3,2,1,0:T(8,128)}), f32[4,4,2,2,128,128]{5,4,3,2,1,0:T(8,128)}, u32[]{:S(2)}, u32[]{:S(2)}) async-start(f32[4,4,2,2,128,128]{5,4,3,2,1,0:T(8,128)} %merge.9), calls=%async_computation.2 | async-start | bytes 8388608 | tf_op jit(solution)/shard_map/all_to_all | solution.py:450
  176.3 49.1 %collective-permute-start.11 = (f32[2,904,128]{2,1,0:T(8,128)}, f32[2,904,128]{2,1,0:T(8,128)}, u32[]{:S(2)}, u32[]{:S(2)}) collective-permute-start(f32[2,904,128]{2,1,0:T(8,128)} %get-tuple-element.140), channel_id=1, source_target_pairs={{0,2},{1,3},{2,0},{3,1},{4,6},{5,7},{6,4},{7,5},{8,10},{9,11},{10,... | collective-permute-start | bytes 2777096 | tf_op jit(solution)/shard_map/ppermute | solution.py:447
  186.5 64.1 %collective-permute-start.12 = (f32[2,904,128]{2,1,0:T(8,128)S(1)}, f32[2,904,128]{2,1,0:T(8,128)}, u32[]{:S(2)}, u32[]{:S(2)}) collective-permute-start(f32[2,904,128]{2,1,0:T(8,128)S(1)} %copy-done.19), channel_id=1, source_target_pairs={{0,4},{1,5},{2,6},{3,7},{4,0},{5,1},{6,2},{7,3},{8,12},{9,13},{10,... | collective-permute-start | bytes 2777096 | tf_op jit(solution)/shard_map/ppermute | solution.py:447
  187.6 63.0 %collective-permute-start.13 = (f32[2,904,128]{2,1,0:T(8,128)S(1)}, f32[2,904,128]{2,1,0:T(8,128)}, u32[]{:S(2)}, u32[]{:S(2)}) collective-permute-start(f32[2,904,128]{2,1,0:T(8,128)S(1)} %copy-done.18), channel_id=1, source_target_pairs={{0,6},{1,7},{2,4},{3,5},{4,2},{5,3},{6,0},{7,1},{8,14},{9,15},{10,... | collective-permute-start | bytes 2777096 | tf_op jit(solution)/shard_map/ppermute | solution.py:447
  250.7 25.9 %copy-start.17 = (s32[256]{0:T(256)S(1)}, s32[256]{0:T(256)}, u32[]{:S(2)}) copy-start(s32[256]{0:T(256)} %param.4) | copy-start | bytes 3076
  250.7 87.7 %all-to-all-start.3 = ((f32[4,4,2,2,128,128]{5,4,3,2,1,0:T(8,128)}), f32[4,4,2,2,128,128]{5,4,3,2,1,0:T(8,128)}, u32[]{:S(2)}, u32[]{:S(2)}) async-start(f32[4,4,2,2,128,128]{5,4,3,2,1,0:T(8,128)} %regroup.1), calls=%async_computation.3 | async-start | bytes 8388608 | tf_op jit(solution)/shard_map/all_to_all | solution.py:450
  255.9 55.1 %collective-permute-start.14 = (f32[2,904,128]{2,1,0:T(8,128)}, f32[2,904,128]{2,1,0:T(8,128)S(1)}, u32[]{:S(2)}, u32[]{:S(2)}) collective-permute-start(f32[2,904,128]{2,1,0:T(8,128)} %get-tuple-element.157), channel_id=1, source_target_pairs={{0,2},{1,3},{2,0},{3,1},{4,6},{5,7},{6,4},{7,5},{8,10},{9,11},{10,... | collective-permute-start | bytes 2777096 | tf_op jit(solution)/shard_map/ppermute | solution.py:447
  274.1 64.2 %collective-permute-start.15 = (f32[2,904,128]{2,1,0:T(8,128)}, f32[2,904,128]{2,1,0:T(8,128)S(1)}, u32[]{:S(2)}, u32[]{:S(2)}) collective-permute-start(f32[2,904,128]{2,1,0:T(8,128)} %get-tuple-element.158), channel_id=1, source_target_pairs={{0,4},{1,5},{2,6},{3,7},{4,0},{5,1},{6,2},{7,3},{8,12},{9,13},{10,... | collective-permute-start | bytes 2777096 | tf_op jit(solution)/shard_map/ppermute | solution.py:447
  275.2 63.2 %collective-permute-start.16 = (f32[2,904,128]{2,1,0:T(8,128)}, f32[2,904,128]{2,1,0:T(8,128)S(1)}, u32[]{:S(2)}, u32[]{:S(2)}) collective-permute-start(f32[2,904,128]{2,1,0:T(8,128)} %get-tuple-element.159), channel_id=1, source_target_pairs={{0,6},{1,7},{2,4},{3,5},{4,2},{5,3},{6,0},{7,1},{8,14},{9,15},{10,... | collective-permute-start | bytes 2777096 | tf_op jit(solution)/shard_map/ppermute | solution.py:447
  311.0 68.6 %copy-start.7 = (f32[2,904,128]{2,1,0:T(8,128)}, f32[2,904,128]{2,1,0:T(8,128)S(1)}, u32[]{:S(2)}) copy-start(f32[2,904,128]{2,1,0:T(8,128)S(1)} %collective-permute-done.14.refs_1_) | copy-start | bytes 2777092
  338.4 41.2 %copy-start.8 = (f32[2,904,128]{2,1,0:T(8,128)}, f32[2,904,128]{2,1,0:T(8,128)S(1)}, u32[]{:S(2)}) copy-start(f32[2,904,128]{2,1,0:T(8,128)S(1)} %collective-permute-done.15.refs_2_) | copy-start | bytes 2777092
  338.4 41.2 %copy-start.9 = (f32[2,904,128]{2,1,0:T(8,128)}, f32[2,904,128]{2,1,0:T(8,128)S(1)}, u32[]{:S(2)}) copy-start(f32[2,904,128]{2,1,0:T(8,128)S(1)} %collective-permute-done.16.refs_3_) | copy-start | bytes 2777092
  338.4 62.9 %collective-permute-start.17 = (f32[2,904,128]{2,1,0:T(8,128)}, f32[2,904,128]{2,1,0:T(8,128)S(1)}, u32[]{:S(2)}, u32[]{:S(2)}) collective-permute-start(f32[2,904,128]{2,1,0:T(8,128)} %get-tuple-element.173), channel_id=1, source_target_pairs={{0,2},{1,3},{2,0},{3,1},{4,6},{5,7},{6,4},{7,5},{8,10},{9,11},{10,... | collective-permute-start | bytes 2777096 | tf_op jit(solution)/shard_map/ppermute | solution.py:447
  355.4 64.2 %collective-permute-start.18 = (f32[2,904,128]{2,1,0:T(8,128)}, f32[2,904,128]{2,1,0:T(8,128)S(1)}, u32[]{:S(2)}, u32[]{:S(2)}) collective-permute-start(f32[2,904,128]{2,1,0:T(8,128)} %get-tuple-element.174), channel_id=1, source_target_pairs={{0,4},{1,5},{2,6},{3,7},{4,0},{5,1},{6,2},{7,3},{8,12},{9,13},{10,... | collective-permute-start | bytes 2777096 | tf_op jit(solution)/shard_map/ppermute | solution.py:447
  356.5 63.2 %collective-permute-start.19 = (f32[2,904,128]{2,1,0:T(8,128)}, f32[2,904,128]{2,1,0:T(8,128)S(1)}, u32[]{:S(2)}, u32[]{:S(2)}) collective-permute-start(f32[2,904,128]{2,1,0:T(8,128)} %get-tuple-element.175), channel_id=1, source_target_pairs={{0,6},{1,7},{2,4},{3,5},{4,2},{5,3},{6,0},{7,1},{8,14},{9,15},{10,... | collective-permute-start | bytes 2777096 | tf_op jit(solution)/shard_map/ppermute | solution.py:447
  401.3 18.4 %copy-start.10 = (f32[2,904,128]{2,1,0:T(8,128)}, f32[2,904,128]{2,1,0:T(8,128)S(1)}, u32[]{:S(2)}) copy-start(f32[2,904,128]{2,1,0:T(8,128)S(1)} %collective-permute-done.17.refs_1_) | copy-start | bytes 2777092
  419.6 1.0 copy-start.11
  419.6 1.3 copy-start.12
  472.8 5.8 %copy-start = (f32[8,2,512,512]{3,2,1,0:T(8,128)S(1)}, f32[8,2,512,512]{3,2,1,0:T(8,128)}, u32[]{:S(2)}) copy-start(f32[8,2,512,512]{3,2,1,0:T(8,128)} %get-tuple-element.99.resid_ref) | copy-start | bytes 50331652
  478.6 5.8 %copy-start.1 = (f32[8,2,512,512]{3,2,1,0:T(8,128)S(1)}, f32[8,2,512,512]{3,2,1,0:T(8,128)}, u32[]{:S(2)}) copy-start(f32[8,2,512,512]{3,2,1,0:T(8,128)} %get-tuple-element.199.pred_ref) | copy-start | bytes 50331652
